TPU v7x, 768 devices: a whole 4x8x12 slice. The times are simulated.
768 devices in a mesh: gx: 96 (over z, x, core), yz: 8 (over y).
Axes of the slice: x: 4, y: 8, z: 12, core: 2. Of those that a mesh axis runs over, the one named last changes fastest.
Arguments:
- coarse_state: float32 [21, 576, 48, 384], P(None, 'gx', 'yz')
- fine_state: bfloat16 [6144, 21, 512], P(('gx', 'yz')), may hold values from -6 to 6
- diffusion: float32 [21], replicated, may hold values from 0.005 to 0.04
- rate: float32 [21, 21], replicated, may hold values from -0.625 to 0.625
- box_pos: int32 [96, 8, 4], P('gx', 'yz'), may hold values from 0 to 63, as said below
- box_owner: int32 [96, 8, 4], P('gx', 'yz'), may hold values from 0 to 7, as said below
Outputs:
- coarse_next: float32 [21, 576, 48, 384], P(None, 'gx', 'yz')
- fine_next: bfloat16 [6144, 21, 512], P(('gx', 'yz'))
Inputs may be any that keep to these rules, and one draw needn't show every extreme that they name: `box_pos`: the 4 positions of one device are distinct. `box_owner`: the 4 boxes of one device go to distinct owners of its slab; in every slab some owner receives a box from every device of the slab.
All inputs are finite; a program needn't handle non-finite values.
Results may differ from a plain program's by a relative error of at most 0.0025.
Values may be sent and summed in bfloat16 or wider, within the bound.
A program may use at most 64 MiB of HBM per device.

v0:
```python
import functools

import jax
import jax.numpy as jnp
import numpy as np
from jax import lax
from jax.experimental import pallas as pl
from jax.experimental.pallas import tpu as pltpu
from jax.sharding import PartitionSpec as P

S = 21
BF = jnp.bfloat16
F32 = jnp.float32
SP = 24
ROWS = 6 * SP
NZ = 384
PATCH = 384
FINE = 512
WIDE = 4 * SP


def constants():
    fine = [(x, y, z) for x in range(8) for y in range(8) for z in range(8)]
    touch = np.zeros((PATCH, FINE), np.float32)
    lap = np.zeros((FINE, FINE), np.float32)
    mean = np.zeros((FINE, PATCH), np.float32)
    for cell, at in enumerate(fine):
        lap[cell, cell] = -6.0
        inner = [c // 2 + 1 for c in at]
        mean[cell, inner[0] * 64 + inner[1] * 8 + inner[2]] = 0.125
        for axis, stride in enumerate((64, 8, 1)):
            for step, edge, ghost in ((-1, 0, 0), (1, 7, 5)):
                if at[axis] == edge:
                    cyc = list(inner)
                    cyc[axis] = ghost
                    touch[cyc[0] * 64 + cyc[1] * 8 + cyc[2], cell] = 1.0
                else:
                    lap[cell + step * stride, cell] = 1.0
    face = np.zeros((PATCH, PATCH), np.float32)
    for a in range(1, 5):
        for b in range(1, 5):
            for axis in range(3):
                for low, inner in ((0, 1), (5, 4)):
                    at = [a, b]
                    at.insert(axis, low)
                    near = [a, b]
                    near.insert(axis, inner)
                    q = at[0] * 64 + at[1] * 8 + at[2]
                    face[q, q] = 1.0
                    face[near[0] * 64 + near[1] * 8 + near[2], q] = -1.0
    lap_pool = np.concatenate([lap, 0.25 * touch.T], axis=1)
    return (lap_pool, touch, mean, face)


def iota(shape, dim):
    return lax.broadcasted_iota(jnp.int32, shape, dim)


def dot(a, b):
    return jnp.dot(a, b, preferred_element_type=F32)


def one(mask, kind=BF):
    return jnp.where(mask, 1.0, 0.0).astype(kind)


def split(value):
    high = value.astype(BF)
    return high, (value - high.astype(F32)).astype(BF)


def kernel(
    n_gx,
    n_yz,
    coarse,
    fine,
    diffusion,
    rate,
    box_pos,
    box_owner,
    lap_pool_in,
    touch_in,
    mean_in,
    face_in,
    coarse_out,
    fine_out,
    cv,
    fv,
    lap_pool,
    touch,
    mean,
    face,
    rz,
    xf,
    xh,
    adv,
    ysend,
    yrecv,
    xrecv,
    packed,
    fbuf,
    sbuf,
    rbuf,
    ov,
    load_sem,
    own_sem,
    halo_send,
    halo_recv,
    fine_send,
    fine_recv,
    back_send,
    back_recv,
    out_sem,
):
    gx = lax.axis_index("gx")
    me = lax.axis_index("yz")
    right, left = lax.rem(gx + 1, n_gx), lax.rem(gx + n_gx - 1, n_gx)
    up, down = lax.rem(me + 1, n_yz), lax.rem(me + n_yz - 1, n_yz)
    mesh_id = pl.DeviceIdType.MESH

    loads = [
        pltpu.make_async_copy(coarse, cv, load_sem.at[0]),
        pltpu.make_async_copy(fine, fv, load_sem.at[1]),
        pltpu.make_async_copy(lap_pool_in, lap_pool, load_sem.at[2]),
        pltpu.make_async_copy(touch_in, touch, load_sem.at[3]),
        pltpu.make_async_copy(mean_in, mean, load_sem.at[4]),
        pltpu.make_async_copy(face_in, face, load_sem.at[5]),
    ]
    for copy in loads:
        copy.start()

    barrier = pltpu.get_barrier_semaphore()
    for step in range(1, n_yz):
        pl.semaphore_signal(
            barrier, inc=1, device_id=(gx, lax.rem(me + step, n_yz)), device_id_type=mesh_id
        )
    for other in (left, right):
        pl.semaphore_signal(barrier, inc=1, device_id=(other, me), device_id_type=mesh_id)

    loads[0].wait()
    for x in range(6):
        value = jnp.concatenate([cv[x], jnp.zeros((6, SP - S, NZ), F32)], axis=1)
        value = value.reshape(ROWS, NZ)
        xf[x] = value
        xh[x] = value.astype(BF)
        if x % 2:
            before = xf[x - 1]
            first = jnp.concatenate([before[:SP], value[:SP]], axis=0)
            last = jnp.concatenate([before[ROWS - SP :], value[ROWS - SP :]], axis=0)
            ysend[0, x // 2] = first.astype(BF)
            ysend[1, x // 2] = last.astype(BF)

    loads[1].wait()
    slots = fv[...].astype(F32).reshape(S * 8, FINE)
    slots = jnp.concatenate([slots, jnp.zeros((8, FINE), F32)], axis=0).astype(BF)
    row = iota((8, SP, S * 8 + 8), 1) * 8 + iota((8, SP, S * 8 + 8), 0)
    order = one(row == iota((8, SP, S * 8 + 8), 2), F32).reshape(8 * SP, S * 8 + 8)
    slots = dot(order.astype(BF), slots)
    for j in range(8):
        value = slots[j * SP : (j + 1) * SP]
        value = jnp.concatenate([value[:, : FINE // 2], value[:, FINE // 2 :]], axis=0)
        packed[j] = value.astype(BF)

    pl.semaphore_wait(barrier, n_yz + 1)

    def remote(src, dst, sends, recvs, at, target):
        return pltpu.make_async_remote_copy(
            src_ref=src,
            dst_ref=dst,
            send_sem=sends.at[at],
            recv_sem=recvs.at[at],
            device_id=target,
            device_id_type=mesh_id,
        )

    halos = [
        remote(ysend.at[0], yrecv.at[1], halo_send, halo_recv, 0, (gx, down)),
        remote(ysend.at[1], yrecv.at[0], halo_send, halo_recv, 1, (gx, up)),
        remote(xh.at[0], xrecv.at[1], halo_send, halo_recv, 2, (left, me)),
        remote(xh.at[5], xrecv.at[0], halo_send, halo_recv, 3, (right, me)),
    ]
    for copy in halos:
        copy.start()
    gathers = []
    for step in (4, 3, 5, 2, 6, 1, 7):
        host = lax.rem(me + step, n_yz)
        gathers.append(
            remote(packed.at[host], fbuf.at[me], fine_send, fine_recv, step, (gx, host))
        )
        gathers[-1].start()
    mine = pltpu.make_async_copy(packed.at[me], fbuf.at[me], own_sem.at[0])
    mine.start()

    rz[...] = jnp.zeros_like(rz)
    rz[0:S, 0:S] = rate[...]
    rate_high, rate_low = split(rz[...])

    def repeated(count):
        at = iota((count, SP, 128), 1)
        return one(at == iota((count, SP, 128), 2), F32).reshape(count * SP, 128).astype(BF)

    def group(count):
        return iota((count, SP, 1), 0).astype(F32).reshape(count * SP, 1)

    def group_lane(count):
        lane = iota((1, count * SP), 1)
        at = jnp.zeros((1, count * SP), jnp.int32)
        for i in range(1, count):
            at = at + jnp.where(lane >= i * SP, 1, 0)
        return at.astype(F32)

    def blocks(count, part):
        tall = repeated(count)
        full = lax.dot_general(
            dot(tall, part).astype(BF), tall, (((1,), (1,)), ((), ())), preferred_element_type=F32
        )
        return jnp.where(group(count) == group_lane(count), full, 0.0)

    mix_high = blocks(6, rate_high).astype(BF)
    mix_low = blocks(6, rate_low).astype(BF)
    box_high = (0.5 * blocks(4, rate_high)).astype(BF)
    box_low = (0.5 * blocks(4, rate_low)).astype(BF)
    at = iota((SP, 1), 0)
    column = jnp.zeros((SP, 1), F32)
    for s in range(S):
        column = jnp.where(at == s, diffusion[s], column)
    d_slab = jnp.concatenate([column] * 6, axis=0)
    d_box = jnp.concatenate([column] * 4, axis=0)

    def start_of(index):
        place = jnp.full(index.shape, box_pos[0, 0, 0] * 6, jnp.int32)
        for i in range(1, 4):
            place = jnp.where(index == i, box_pos[0, 0, i] * 6, place)
        return place

    lane = iota((1, 256), 1)
    want = jnp.where((lane & 7) < 6, start_of(lane >> 6) + (lane & 7), -1)
    take = one(iota((NZ, 256), 0) == want)
    lane = iota((256, 1), 0)
    want = jnp.where((lane & 7) < 6, start_of(lane >> 6) + (lane & 7), -1)
    give = one(iota((256, NZ), 1) == want)
    y_lane = (iota((1, 256), 1) >> 3) & 7

    def to_patch(slab):
        cells = dot(slab, take)
        patch = jnp.zeros((SP, 256), F32)
        for y in range(6):
            patch = jnp.where(y_lane == y, cells[y * SP : (y + 1) * SP], patch)
        return patch

    def by_box(parts):
        rows = [
            jnp.concatenate([part[:, i * 64 : (i + 1) * 64] for part in parts], axis=1)
            for i in range(4)
        ]
        return jnp.concatenate(rows, axis=0)

    olds = []
    for x in range(6):
        value = xf[x]
        high = xh[x]
        low = (value - high.astype(F32)).astype(BF)
        around = pltpu.roll(value, 1, 1) + pltpu.roll(value, NZ - 1, 1) - 6.0 * value
        if x > 0:
            around = around + xf[x - 1]
        if x < 5:
            around = around + xf[x + 1]
        rest = jnp.zeros((SP, NZ), F32)
        around = around + jnp.concatenate([rest, value[: ROWS - SP]], axis=0)
        around = around + jnp.concatenate([value[SP:], rest], axis=0)
        mixed = dot(mix_high, high) + dot(mix_low, high) + dot(mix_high, low)
        adv[x] = value + mixed + d_slab * around
        olds.append(to_patch(high))
    old = by_box(olds)

    for copy in halos:
        copy.wait_recv()
    news = []
    rest = jnp.zeros((ROWS - 2 * SP, NZ), F32)
    for pair in range(3):
        before = yrecv[0, pair].astype(F32)
        after = yrecv[1, pair].astype(F32)
        for k in range(2):
            x = 2 * pair + k
            part = slice(k * SP, (k + 1) * SP)
            around = jnp.concatenate([before[part], rest, after[part]], axis=0)
            if x == 0:
                around = around + xrecv[0].astype(F32)
            if x == 5:
                around = around + xrecv[1].astype(F32)
            value = adv[x] + d_slab * around
            adv[x] = value
            news.append(to_patch(value.astype(BF)))
    new = by_box(news)

    for copy in loads[2:]:
        copy.wait()
    ghost_old = dot(old.astype(BF), touch[...])
    ghost_mid = 0.5 * (ghost_old + dot(new.astype(BF), touch[...]))
    for copy in gathers:
        copy.wait_recv()
    mine.wait()
    boxes = []
    for i in range(4):
        value = fbuf[box_owner[0, 0, i]].astype(F32)
        boxes.append(jnp.concatenate([value[:SP], value[SP:]], axis=1))
    field = jnp.concatenate(boxes, axis=0)
    high = field.astype(BF)
    both = dot(high, lap_pool[...])
    pooled = both[:, FINE:]
    field = (
        field
        + (2.0 * d_box) * (both[:, :FINE] + ghost_old)
        + (dot(box_high, high) + dot(box_low, high))
    )
    high, low = split(field)
    both = dot(high, lap_pool[...]) + dot(low, lap_pool[...])
    pooled = pooled + both[:, FINE:]
    field = (
        field
        + (2.0 * d_box) * (both[:, :FINE] + ghost_mid)
        + (dot(box_high, high) + dot(box_low, high) + dot(box_high, low))
    )

    for owner in range(8):
        slot = jnp.zeros((SP, FINE), F32)
        for i in range(4):
            sent = box_owner[0, 0, i] == owner
            slot = slot + jnp.where(sent, field[i * SP : (i + 1) * SP], 0.0)
        slot = jnp.concatenate([slot[:, : FINE // 2], slot[:, FINE // 2 :]], axis=0)
        sbuf[owner] = slot.astype(BF)
    backs = []
    for step in (4, 3, 5, 2, 6, 1, 7):
        owner = lax.rem(me + step, n_yz)
        backs.append(
            remote(sbuf.at[owner], rbuf.at[me], back_send, back_recv, step, (gx, owner))
        )
        backs[-1].start()
    own = pltpu.make_async_copy(sbuf.at[me], rbuf.at[me], own_sem.at[1])
    own.start()

    lane = iota((1, PATCH), 1)
    parts = [(lane >> 6), (lane >> 3) & 7, lane & 7]
    ends = [jnp.where((part == 0) | (part == 5), 1, 0) for part in parts]
    outside = [jnp.where(part > 5, 1, 0) for part in parts]
    on_face = (ends[0] + ends[1] + ends[2] == 1) & (outside[0] + outside[1] + outside[2] == 0)
    ghosts = jnp.where(on_face, 1.5 * old + 0.5 * new, 0.0)
    delta = d_box * (dot(old.astype(BF), face[...]) - ghosts + pooled)
    delta = delta + dot(field.astype(BF), mean[...])
    zat = iota((1, NZ), 1)
    inside = jnp.zeros((1, NZ), jnp.int32)
    for i in range(4):
        offset = zat - box_pos[0, 0, i] * 6
        inside = inside + jnp.where((offset >= 1) & (offset <= 4), 1, 0)
    stores = []
    for x in range(6):
        part = [delta[i * SP : (i + 1) * SP, x * 64 : (x + 1) * 64] for i in range(4)]
        part = jnp.concatenate(part, axis=1)
        cells = [jnp.where(y_lane == y, part, 0.0) for y in range(6)]
        change = dot(jnp.concatenate(cells, axis=0).astype(BF), give)
        value = adv[x]
        total = value + change
        if 1 <= x <= 4:
            middle = jnp.where(inside > 0, change[SP : ROWS - SP], total[SP : ROWS - SP])
            total = jnp.concatenate([total[:SP], middle, total[ROWS - SP :]], axis=0)
        ov[x] = total.reshape(6, SP, NZ)[:, :S]
        stores.append(pltpu.make_async_copy(ov.at[x], coarse_out.at[x], out_sem.at[x]))
        stores[-1].start()

    row = iota((S, 8, 8 * SP), 1) * SP + iota((S, 8, 8 * SP), 0)
    order = one(row == iota((S, 8, 8 * SP), 2), F32).reshape(S * 8, 8 * SP).astype(BF)
    for copy in backs:
        copy.wait_recv()
    own.wait()
    slots = []
    for j in range(8):
        value = rbuf[j].astype(F32)
        slots.append(jnp.concatenate([value[:SP], value[SP:]], axis=1))
    slots = jnp.concatenate(slots, axis=0).astype(BF)
    fine_out[...] = dot(order, slots).reshape(S, 8, FINE).astype(BF)

    for copy in halos + gathers + backs:
        copy.wait_send()
    for copy in stores:
        copy.wait()


def local(n_gx, n_yz, consts, coarse_state, fine_state, diffusion, rate, box_pos, box_owner):
    hbm = pl.BlockSpec(memory_space=pl.ANY)
    vmem = pl.BlockSpec(memory_space=pltpu.VMEM)
    smem = pl.BlockSpec(memory_space=pltpu.SMEM)
    dma = pltpu.SemaphoreType.DMA
    coarse, fine = pl.pallas_call(
        functools.partial(kernel, n_gx, n_yz),
        out_shape=(
            jax.ShapeDtypeStruct((6, 6, S, NZ), F32),
            jax.ShapeDtypeStruct((S, 8, FINE), BF),
        ),
        in_specs=[hbm, hbm, smem, vmem, smem, smem, hbm, hbm, hbm, hbm],
        out_specs=(hbm, vmem),
        scratch_shapes=[
            pltpu.VMEM((6, 6, S, NZ), F32),
            pltpu.VMEM((S, 8, FINE), BF),
            pltpu.VMEM((FINE, FINE + PATCH), BF),
            pltpu.VMEM((PATCH, FINE), BF),
            pltpu.VMEM((FINE, PATCH), BF),
            pltpu.VMEM((PATCH, PATCH), BF),
            pltpu.VMEM((128, 128), F32),
            pltpu.VMEM((6, ROWS, NZ), F32),
            pltpu.VMEM((6, ROWS, NZ), BF),
            pltpu.VMEM((6, ROWS, NZ), F32),
            pltpu.VMEM((2, 3, 2 * SP, NZ), BF),
            pltpu.VMEM((2, 3, 2 * SP, NZ), BF),
            pltpu.VMEM((2, ROWS, NZ), BF),
            pltpu.VMEM((8, 2 * SP, FINE // 2), BF),
            pltpu.VMEM((8, 2 * SP, FINE // 2), BF),
            pltpu.VMEM((8, 2 * SP, FINE // 2), BF),
            pltpu.VMEM((8, 2 * SP, FINE // 2), BF),
            pltpu.VMEM((6, 6, S, NZ), F32),
            dma((6,)),
            dma((2,)),
            dma((4,)),
            dma((4,)),
            dma((8,)),
            dma((8,)),
            dma((8,)),
            dma((8,)),
            dma((6,)),
        ],
        compiler_params=pltpu.CompilerParams(
            collective_id=0, has_side_effects=True, vmem_limit_bytes=56 * 1024 * 1024
        ),
        name="amr_step",
    )(
        jnp.transpose(coarse_state, (1, 2, 0, 3)),
        jnp.transpose(fine_state, (1, 0, 2)),
        diffusion,
        rate,
        box_pos,
        box_owner,
        *consts,
    )
    return jnp.transpose(coarse, (2, 0, 1, 3)), jnp.transpose(fine, (1, 0, 2))


def solution(mesh):
    in_specs = (
        P(None, "gx", "yz", None),
        P(("gx", "yz"), None, None),
        P(),
        P(),
        P("gx", "yz", None),
        P("gx", "yz", None),
    )
    out_specs = (P(None, "gx", "yz", None), P(("gx", "yz"), None, None))
    consts = [np.asarray(c).astype(jnp.bfloat16) for c in constants()]
    body = functools.partial(local, mesh.shape["gx"], mesh.shape["yz"], consts)
    return jax.shard_map(body, mesh=mesh, in_specs=in_specs, out_specs=out_specs, check_vma=False)
```

profile of v0, /device:TPU:8, one launch (start us, length us, event | category | flops | bytes accessed | tf_op | source)
XLA Modules:
  0.0 37.0 jit_solution(16662099042416990636)
XLA Ops:
  0.6 33.2 %amr_step.1 = (f32[6,6,21,384]{3,2,1,0:T(8,128)}, bf16[21,8,512]{2,1,0:T(8,128)(2,1)}) custom-call(f32[6,6,21,384]{3,2,1,0:T(8,128)} %bitcast.5, bf16[21,8,512]{2,1,0:T(8,128)(2,1)} %bitcast.7, f32[21]{0:T(128)} %diffusion.1, f32[21,21]{1,0:T(8,128)} %rate.1, s32[1,1,4]{2,1,0:T(1,128)} %box_pos.1, s32[1,1,4]{2,1,0:T(1,128)} %box_owner.1, ...), custom_call_target="tpu_custom_call" | custom-call | tf_op jit(solution)/shard_map/amr_step/pallas_call | solution.py:393
  33.8 0.0 copy-start
  33.9 2.5 %copy.14 = f32[21,6,6,384]{3,0,2,1:T(8,128)} copy(f32[21,6,6,384]{3,0,2,1:T(8,128)} %bitcast.4) | data formatting | bytes 2322432
  36.4 0.0 copy-done
  36.4 0.7 %copy.15 = bf16[8,21,512]{2,0,1:T(8,128)(2,1)} copy(bf16[8,21,512]{2,0,1:T(8,128)(2,1)S(1)} %bitcast.6) | data formatting | bytes 344064
Async XLA Ops:
  33.8 2.5 %copy-start = (bf16[21,8,512]{2,1,0:T(8,128)(2,1)S(1)}, bf16[21,8,512]{2,1,0:T(8,128)(2,1)}, u32[]{:S(2)}) copy-start(bf16[21,8,512]{2,1,0:T(8,128)(2,1)} %get-tuple-element.5) | copy-start | bytes 516100
where the time goes:
time: 37.2 us; the launch traced here: 37 us
  Pallas kernels  33.2 us (89%)
  local copies, waits for them, and re-layouts  3.18 us (9%)
  between operations  0.65 us (2%)
    pallas_call x1, Pallas kernels, local(): pl.pallas_call(functools.partial(kernel, n_gx, n_yz), out_shape=(jax.Shap...  33.2 us
    unnamed x4, local copies, waits for them, and re-layouts  3.18 us

commit v1 on v0

v1 whole, which is shorter than its diff:
```python
import functools

import jax
import jax.numpy as jnp
import numpy as np
from jax import lax
from jax.experimental import pallas as pl
from jax.experimental.pallas import tpu as pltpu
from jax.sharding import PartitionSpec as P

S = 21
BF = jnp.bfloat16
F32 = jnp.float32
SP = 24
ROWS = 6 * SP
NZ = 384
PATCH = 384
FINE = 512
SLOT = 176
FACES = 128
FLAG = 21


def constants():
    def patch(at):
        return at[0] * 64 + at[1] * 8 + at[2]

    faces = []
    for axis in range(3):
        for low, inner in ((0, 1), (5, 4)):
            for a in range(1, 5):
                for b in range(1, 5):
                    at, near = [a, b], [a, b]
                    at.insert(axis, low)
                    near.insert(axis, inner)
                    faces.append((tuple(at), tuple(near), axis))
    number = {at: n for n, (at, _, _) in enumerate(faces)}
    touch = np.zeros((FACES, FINE), np.float32)
    lap = np.zeros((FINE, FINE), np.float32)
    mean = np.zeros((FINE, 128), np.float32)
    put_mean = np.zeros((128, PATCH), np.float32)
    cells = [(x, y, z) for x in range(8) for y in range(8) for z in range(8)]
    for cell, at in enumerate(cells):
        lap[cell, cell] = -6.0
        inner = [c // 2 + 1 for c in at]
        box = (inner[0] - 1) * 16 + (inner[1] - 1) * 4 + inner[2] - 1
        mean[cell, box] = 0.125
        put_mean[box, patch(inner)] = 1.0
        for axis, stride in enumerate((64, 8, 1)):
            for step, edge, ghost in ((-1, 0, 0), (1, 7, 5)):
                if at[axis] == edge:
                    cyc = list(inner)
                    cyc[axis] = ghost
                    touch[number[tuple(cyc)], cell] = 1.0
                else:
                    lap[cell + step * stride, cell] = 1.0
    lap_pool = np.concatenate([lap, 0.25 * touch.T], axis=1)
    ghosts = np.zeros((2 * PATCH, 2 * FACES), np.float32)
    fixes = np.zeros((2 * PATCH, PATCH), np.float32)
    put_face = np.zeros((FACES, PATCH), np.float32)
    sides = np.zeros((256, FACES), np.float32)
    for n, (at, near, axis) in enumerate(faces):
        q = patch(at)
        ghosts[q, n] = 1.0
        ghosts[PATCH + q, FACES + n] = 1.0
        fixes[q, q] = 1.0 - 1.5
        fixes[patch(near), q] = -1.0
        fixes[PATCH + q, q] = -0.5
        put_face[n, q] = 1.0
        if n < 64:
            rest = [at[d] for d in range(3) if d != axis]
            sides[n // 16 * 64 + rest[0] * 8 + rest[1], n] = 1.0
    late = (touch @ mean @ put_mean) - 0.5 * put_face
    late[64:] = 0.0
    return (lap_pool, touch, mean, ghosts, fixes, put_face, put_mean, sides, late)


def iota(shape, dim):
    return lax.broadcasted_iota(jnp.int32, shape, dim)


def dot(a, b):
    return jnp.dot(a, b, preferred_element_type=F32)


def dot_nt(a, b):
    return lax.dot_general(a, b, (((1,), (1,)), ((), ())), preferred_element_type=F32)


def one(mask, kind=BF):
    return jnp.where(mask, 1.0, 0.0).astype(kind)


def split(value):
    high = value.astype(BF)
    return high, (value - high.astype(F32)).astype(BF)


def fold(value):
    half = value.shape[1] // 2
    return jnp.concatenate([value[:, :half], value[:, half:]], axis=0)


def unfold(value):
    value = value.astype(F32)
    return jnp.concatenate([value[:SP], value[SP:]], axis=1)


def kernel(
    n_gx,
    n_yz,
    coarse,
    fine,
    diffusion,
    rate,
    box_pos,
    box_owner,
    lap_pool_in,
    touch_in,
    mean_in,
    ghosts_in,
    fixes_in,
    put_face_in,
    put_mean_in,
    sides_in,
    late_in,
    coarse_out,
    fine_out,
    cv,
    fv,
    lap_pool,
    touch,
    mean,
    ghosts,
    fixes,
    put_face,
    put_mean,
    sides,
    late,
    rz,
    xf,
    xh,
    adv,
    ysend,
    yrecv,
    xrecv,
    ghost_out,
    ghost_in,
    back_out,
    back_in,
    late_out,
    late_got,
    ov,
    load_sem,
    own_sem,
    halo_send,
    halo_recv,
    ghost_send,
    ghost_recv,
    back_send,
    back_recv,
    late_send,
    late_recv,
    out_sem,
    ready,
):
    gx = lax.axis_index("gx")
    me = lax.axis_index("yz")
    right, left = lax.rem(gx + 1, n_gx), lax.rem(gx + n_gx - 1, n_gx)
    up, down = lax.rem(me + 1, n_yz), lax.rem(me + n_yz - 1, n_yz)
    mesh_id = pl.DeviceIdType.MESH

    barrier = pltpu.get_barrier_semaphore()
    for step in range(1, n_yz):
        pl.semaphore_signal(
            barrier, inc=1, device_id=(gx, lax.rem(me + step, n_yz)), device_id_type=mesh_id
        )
    pl.semaphore_signal(barrier, inc=1, device_id=(left, me), device_id_type=mesh_id)

    loads = [
        pltpu.make_async_copy(src, dst, load_sem.at[n])
        for n, (src, dst) in enumerate(
            [
                (coarse, cv),
                (fine, fv),
                (lap_pool_in, lap_pool),
                (touch_in, touch),
                (mean_in, mean),
                (ghosts_in, ghosts),
                (fixes_in, fixes),
                (put_face_in, put_face),
                (put_mean_in, put_mean),
                (sides_in, sides),
                (late_in, late),
            ]
        )
    ]
    for copy in loads:
        copy.start()

    def remote(src, dst, sends, recvs, at, target):
        return pltpu.make_async_remote_copy(
            src_ref=src,
            dst_ref=dst,
            send_sem=sends.at[at],
            recv_sem=recvs.at[at],
            device_id=target,
            device_id_type=mesh_id,
        )

    def exchange(out, got, sends, recvs, n):
        copies = []
        for step in (4, 3, 5, 2, 6, 1, 7):
            other = lax.rem(me + step, n_yz)
            copies.append(remote(out.at[other], got.at[me], sends, recvs, step, (gx, other)))
            copies[-1].start()
        own = pltpu.make_async_copy(out.at[me], got.at[me], own_sem.at[n])
        own.start()
        return copies, own

    loads[0].wait()
    for x in range(6):
        value = jnp.concatenate([cv[x], jnp.zeros((6, SP - S, NZ), F32)], axis=1)
        value = value.reshape(ROWS, NZ)
        xf[x] = value
        xh[x] = value.astype(BF)
        if x % 2:
            before = xf[x - 1]
            first = jnp.concatenate([before[:SP], value[:SP]], axis=0)
            last = jnp.concatenate([before[ROWS - SP :], value[ROWS - SP :]], axis=0)
            ysend[0, x // 2] = first.astype(BF)
            ysend[1, x // 2] = last.astype(BF)

    pl.semaphore_wait(barrier, n_yz)
    pl.semaphore_signal(ready, inc=1, device_id=(right, me), device_id_type=mesh_id)
    to_right = remote(xh.at[5], xrecv.at[0], halo_send, halo_recv, 0, (right, me))
    to_left = remote(xh.at[0], xrecv.at[1], halo_send, halo_recv, 1, (left, me))
    to_down = remote(ysend.at[0], yrecv.at[1], halo_send, halo_recv, 2, (gx, down))
    to_up = remote(ysend.at[1], yrecv.at[0], halo_send, halo_recv, 3, (gx, up))
    to_right.start()
    to_down.start()
    to_up.start()

    rz[...] = jnp.zeros_like(rz)
    rz[0:S, 0:S] = rate[...]
    rate_high, rate_low = split(rz[...])
    tall = one(iota((6, SP, 128), 1) == iota((6, SP, 128), 2), F32)
    tall = tall.reshape(ROWS, 128).astype(BF)
    y_row = iota((6, SP, 1), 0).astype(F32).reshape(ROWS, 1)
    lane = iota((1, ROWS), 1)
    y_col = jnp.zeros((1, ROWS), F32)
    for y in range(1, 6):
        y_col = y_col + jnp.where(lane >= y * SP, 1.0, 0.0)

    def mix(part):
        full = dot_nt(dot(tall, part).astype(BF), tall)
        return jnp.where(y_row == y_col, full, 0.0).astype(BF)

    mix_high, mix_low = mix(rate_high), mix(rate_low)
    at = iota((SP, 1), 0)
    column = jnp.zeros((SP, 1), F32)
    for s in range(S):
        column = jnp.where(at == s, diffusion[s], column)
    d_slab = jnp.concatenate([column] * 6, axis=0)
    d_box = jnp.concatenate([column] * 4, axis=0)

    def start_of(index):
        place = jnp.full(index.shape, box_pos[0, 0, 0] * 6, jnp.int32)
        for i in range(1, 4):
            place = jnp.where(index == i, box_pos[0, 0, i] * 6, place)
        return place

    lane = iota((1, 256), 1)
    want = jnp.where((lane & 7) < 6, start_of(lane >> 6) + (lane & 7), -1)
    take = one(iota((NZ, 256), 0) == want)
    y_lane = (iota((1, 256), 1) >> 3) & 7

    def to_patch(slab):
        cells = dot(slab, take)
        patch = jnp.zeros((SP, 256), F32)
        for y in range(6):
            patch = jnp.where(y_lane == y, cells[y * SP : (y + 1) * SP], patch)
        return patch

    def by_box(parts):
        rows = [
            jnp.concatenate([part[:, i * 64 : (i + 1) * 64] for part in parts], axis=1)
            for i in range(4)
        ]
        return jnp.concatenate(rows, axis=0)

    def for_owner(value, owner):
        total = jnp.zeros((SP, value.shape[1]), F32)
        for i in range(4):
            sent = box_owner[0, 0, i] == owner
            total = total + jnp.where(sent, value[i * SP : (i + 1) * SP], 0.0)
        return total

    olds, news = [], []
    for x in range(6):
        value = xf[x]
        high = xh[x]
        low = (value - high.astype(F32)).astype(BF)
        around = pltpu.roll(value, 1, 1) + pltpu.roll(value, NZ - 1, 1) - 6.0 * value
        if x > 0:
            around = around + xf[x - 1]
        if x < 5:
            around = around + xf[x + 1]
        rest = jnp.zeros((SP, NZ), F32)
        around = around + jnp.concatenate([rest, value[: ROWS - SP]], axis=0)
        around = around + jnp.concatenate([value[SP:], rest], axis=0)
        mixed = dot(mix_high, high) + dot(mix_low, high) + dot(mix_high, low)
        value = value + mixed + d_slab * around
        adv[x] = value
        olds.append(to_patch(high))
        news.append(to_patch(value.astype(BF)))
    patches = jnp.concatenate([by_box(olds), by_box(news)], axis=1).astype(BF)
    for n in (5, 6):
        loads[n].wait()
    sent = dot(patches, ghosts[...])
    flag = jnp.concatenate([one(at == FLAG, F32)] * 4, axis=0)
    sent = sent + flag
    for owner in range(8):
        ghost_out[owner] = fold(for_owner(sent, owner)).astype(BF)
    ghost_copies, own_ghost = exchange(ghost_out, ghost_in, ghost_send, ghost_recv, 0)

    for n in (1, 2, 3, 4):
        loads[n].wait()
    field = fv[...].astype(F32).reshape(S * 8, FINE)
    field = jnp.concatenate([field, jnp.zeros((8, FINE), F32)], axis=0)
    tall = one((iota((SLOT, 128), 0) >> 3) == iota((SLOT, 128), 1))
    slot_same = (iota((SLOT, SLOT), 0) & 7) == (iota((SLOT, SLOT), 1) & 7)

    def slot_rate(part):
        full = dot_nt(dot(tall, part).astype(BF), tall)
        return jnp.where(slot_same, 0.5 * full, 0.0).astype(BF)

    slot_high, slot_low = slot_rate(rate_high), slot_rate(rate_low)
    d_slot = [jnp.full((8, 1), diffusion[s], F32) for s in range(S)]
    d_slot = jnp.concatenate(d_slot + [jnp.zeros((8, 1), F32)], axis=0)
    row = iota((SLOT, 8 * SP), 0)
    inward = one(iota((SLOT, 8 * SP), 1) == (row & 7) * SP + (row >> 3))
    row = iota((8, SP, SLOT), 1) * 8 + iota((8, SP, SLOT), 0)
    outward = (row == iota((8, SP, SLOT), 2)) & (iota((8, SP, SLOT), 1) < S)
    outward = one(outward, F32).reshape(8 * SP, SLOT).astype(BF)
    high = field.astype(BF)
    both = dot(high, lap_pool[...])
    pooled = both[:, FINE:]
    field = (
        field + (2.0 * d_slot) * both[:, :FINE] + (dot(slot_high, high) + dot(slot_low, high))
    )

    for copy in ghost_copies:
        copy.wait_recv()
    own_ghost.wait()
    pl.semaphore_wait(ready, 1)
    to_left.start()

    got = jnp.concatenate([unfold(ghost_in[j]) for j in range(8)], axis=0).astype(BF)
    got = dot(inward, got)
    used = jnp.concatenate([got[S * 8 :, 0:1]] * (SLOT // 8), axis=0) > 0.5
    got = got.astype(BF)
    ghost_old = dot(got[:, :FACES], touch[...])
    ghost_mid = 0.5 * (ghost_old + dot(got[:, FACES:], touch[...]))
    field = field + (2.0 * d_slot) * ghost_old
    high, low = split(field)
    both = dot(high, lap_pool[...]) + dot(low, lap_pool[...])
    pooled = pooled + both[:, FINE:]
    field = (
        field
        + (2.0 * d_slot) * (both[:, :FINE] + ghost_mid)
        + (dot(slot_high, high) + dot(slot_low, high) + dot(slot_high, low))
    )
    back = jnp.concatenate([pooled, dot(field.astype(BF), mean[...])], axis=1)
    back = dot(outward, back.astype(BF))
    for host in range(8):
        back_out[host] = fold(back[host * SP : (host + 1) * SP]).astype(BF)
    back_copies, own_back = exchange(back_out, back_in, back_send, back_recv, 1)

    for n in (7, 8, 9, 10):
        loads[n].wait()
    for copy in (to_down, to_up, to_left, to_right):
        copy.wait_recv()
    layers = [
        xrecv[0],
        xrecv[1],
        jnp.concatenate([yrecv[0, pair] for pair in range(3)], axis=0),
        jnp.concatenate([yrecv[1, pair] for pair in range(3)], axis=0),
    ]
    added = by_box([to_patch(layer) for layer in layers]).astype(BF)
    added = dot(added, sides[...])
    for owner in range(8):
        part = for_owner(added, owner)
        first = jnp.concatenate([part[0:8, :64], part[8:16, :64]], axis=1)
        last = jnp.concatenate([part[16:24, :64], jnp.zeros((8, 64), F32)], axis=1)
        late_out[owner] = jnp.concatenate([first, last], axis=0).astype(BF)
    late_copies, own_late = exchange(late_out, late_got, late_send, late_recv, 2)

    lane = iota((256, 1), 0)
    want = jnp.where((lane & 7) < 6, start_of(lane >> 6) + (lane & 7), -1)
    give = one(iota((256, NZ), 1) == want)
    delta = dot(patches, fixes[...])
    delta = delta + d_box * dot(added.astype(BF), late[...])
    for copy in back_copies:
        copy.wait_recv()
    own_back.wait()
    mine = [unfold(back_in[box_owner[0, 0, i]]) for i in range(4)]
    mine = jnp.concatenate(mine, axis=0).astype(BF)
    delta = d_box * (delta + dot(mine[:, :FACES], put_face[...]))
    delta = delta + dot(mine[:, FACES:], put_mean[...])
    zat = iota((1, NZ), 1)
    inside = jnp.zeros((1, NZ), jnp.int32)
    for i in range(4):
        offset = zat - box_pos[0, 0, i] * 6
        inside = inside + jnp.where((offset >= 1) & (offset <= 4), 1, 0)
    stores = []
    rest = jnp.zeros((ROWS - 2 * SP, NZ), F32)
    for x in range(6):
        part = slice((x % 2) * SP, (x % 2 + 1) * SP)
        before = yrecv[0, x // 2].astype(F32)[part]
        after = yrecv[1, x // 2].astype(F32)[part]
        around = jnp.concatenate([before, rest, after], axis=0)
        if x == 0:
            around = around + xrecv[0].astype(F32)
        if x == 5:
            around = around + xrecv[1].astype(F32)
        part = [delta[i * SP : (i + 1) * SP, x * 64 : (x + 1) * 64] for i in range(4)]
        part = jnp.concatenate(part, axis=1)
        cells = [jnp.where(y_lane == y, part, 0.0) for y in range(6)]
        change = dot(jnp.concatenate(cells, axis=0).astype(BF), give)
        total = adv[x] + d_slab * around + change
        if 1 <= x <= 4:
            middle = jnp.where(inside > 0, change[SP : ROWS - SP], total[SP : ROWS - SP])
            total = jnp.concatenate([total[:SP], middle, total[ROWS - SP :]], axis=0)
        ov[x] = total.reshape(6, SP, NZ)[:, :S]
        stores.append(pltpu.make_async_copy(ov.at[x], coarse_out.at[x], out_sem.at[x]))
        stores[-1].start()

    for copy in late_copies:
        copy.wait_recv()
    own_late.wait()
    parts = []
    for j in range(8):
        value = late_got[j].astype(F32)
        parts += [value[:8, :64], value[:8, 64:], value[8:, :64]]
    got = dot(inward, jnp.concatenate(parts, axis=0).astype(BF)).astype(BF)
    field = field + (d_slot * d_slot) * dot(got, touch[0:64])
    field = jnp.where(used, field, 0.0)
    fine_out[...] = field[: S * 8].reshape(S, 8, FINE).astype(BF)

    for copy in [to_right, to_left, to_down, to_up] + ghost_copies + back_copies + late_copies:
        copy.wait_send()
    for copy in stores:
        copy.wait()


def local(n_gx, n_yz, consts, coarse_state, fine_state, diffusion, rate, box_pos, box_owner):
    hbm = pl.BlockSpec(memory_space=pl.ANY)
    vmem = pl.BlockSpec(memory_space=pltpu.VMEM)
    smem = pl.BlockSpec(memory_space=pltpu.SMEM)
    dma = pltpu.SemaphoreType.DMA
    coarse, fine = pl.pallas_call(
        functools.partial(kernel, n_gx, n_yz),
        out_shape=(
            jax.ShapeDtypeStruct((6, 6, S, NZ), F32),
            jax.ShapeDtypeStruct((S, 8, FINE), BF),
        ),
        in_specs=[hbm, hbm, smem, vmem, smem, smem] + [hbm] * len(consts),
        out_specs=(hbm, vmem),
        scratch_shapes=[
            pltpu.VMEM((6, 6, S, NZ), F32),
            pltpu.VMEM((S, 8, FINE), BF),
            *[pltpu.VMEM(c.shape, BF) for c in consts],
            pltpu.VMEM((128, 128), F32),
            pltpu.VMEM((6, ROWS, NZ), F32),
            pltpu.VMEM((6, ROWS, NZ), BF),
            pltpu.VMEM((6, ROWS, NZ), F32),
            pltpu.VMEM((2, 3, 2 * SP, NZ), BF),
            pltpu.VMEM((2, 3, 2 * SP, NZ), BF),
            pltpu.VMEM((2, ROWS, NZ), BF),
            *[pltpu.VMEM((8, 2 * SP, 128), BF)] * 4,
            *[pltpu.VMEM((8, 16, 128), BF)] * 2,
            pltpu.VMEM((6, 6, S, NZ), F32),
            dma((2 + len(consts),)),
            dma((3,)),
            dma((4,)),
            dma((4,)),
            *[dma((8,))] * 6,
            dma((6,)),
            pltpu.SemaphoreType.REGULAR,
        ],
        compiler_params=pltpu.CompilerParams(
            collective_id=0, has_side_effects=True, vmem_limit_bytes=56 * 1024 * 1024
        ),
        name="amr_step",
    )(
        jnp.transpose(coarse_state, (1, 2, 0, 3)),
        jnp.transpose(fine_state, (1, 0, 2)),
        diffusion,
        rate,
        box_pos,
        box_owner,
        *consts,
    )
    return jnp.transpose(coarse, (2, 0, 1, 3)), jnp.transpose(fine, (1, 0, 2))


def solution(mesh):
    in_specs = (
        P(None, "gx", "yz", None),
        P(("gx", "yz"), None, None),
        P(),
        P(),
        P("gx", "yz", None),
        P("gx", "yz", None),
    )
    out_specs = (P(None, "gx", "yz", None), P(("gx", "yz"), None, None))
    consts = [np.asarray(c).astype(jnp.bfloat16) for c in constants()]
    body = functools.partial(local, mesh.shape["gx"], mesh.shape["yz"], consts)
    return jax.shard_map(body, mesh=mesh, in_specs=in_specs, out_specs=out_specs, check_vma=False)
```

time: 37.2 us -> 32.8 us (0.88)
  Pallas kernels: 33.2 us -> 28.8 us
    pallas_call x1, Pallas kernels: 33.2 us -> 28.8 us  [local(): pl.pallas_call(functools.partial(kernel, n_gx, n_yz), out_shape=(jax.Shap...]
where the time goes in v1:
time: 32.8 us; the launch traced here: 32.6 us
  Pallas kernels  28.8 us (88%)
  local copies, waits for them, and re-layouts  3.18 us (10%)
  between operations  0.65 us (2%)
    pallas_call x1, Pallas kernels, local(): pl.pallas_call(functools.partial(kernel, n_gx, n_yz), out_shape=(jax.Shap...  28.8 us
    unnamed x4, local copies, waits for them, and re-layouts  3.18 us

profile of v1, /device:TPU:8, one launch (start us, length us, event | category | flops | bytes accessed | tf_op | source)
XLA Modules:
  0.0 32.6 jit_solution(2288923673921375095)
XLA Ops:
  0.6 28.8 %amr_step.1 = (f32[6,6,21,384]{3,2,1,0:T(8,128)}, bf16[21,8,512]{2,1,0:T(8,128)(2,1)}) custom-call(f32[6,6,21,384]{3,2,1,0:T(8,128)} %bitcast.5, bf16[21,8,512]{2,1,0:T(8,128)(2,1)} %bitcast.7, f32[21]{0:T(128)} %diffusion.1, f32[21,21]{1,0:T(8,128)} %rate.1, s32[1,1,4]{2,1,0:T(1,128)} %box_pos.1, s32[1,1,4]{2,1,0:T(1,128)} %box_owner.1, ...), custom_call_target="tpu_custom_call" | custom-call | tf_op jit(solution)/shard_map/amr_step/pallas_call | solution.py:462
  29.4 0.0 copy-start
  29.4 2.5 %copy.19 = f32[21,6,6,384]{3,0,2,1:T(8,128)} copy(f32[21,6,6,384]{3,0,2,1:T(8,128)} %bitcast.4) | data formatting | bytes 2322432
  31.9 0.0 copy-done
  31.9 0.7 %copy.20 = bf16[8,21,512]{2,0,1:T(8,128)(2,1)} copy(bf16[8,21,512]{2,0,1:T(8,128)(2,1)S(1)} %bitcast.6) | data formatting | bytes 344064
Async XLA Ops:
  29.4 2.5 %copy-start = (bf16[21,8,512]{2,1,0:T(8,128)(2,1)S(1)}, bf16[21,8,512]{2,1,0:T(8,128)(2,1)}, u32[]{:S(2)}) copy-start(bf16[21,8,512]{2,1,0:T(8,128)(2,1)} %get-tuple-element.5) | copy-start | bytes 516100

commit v2 on v1

--- a/solution.py
+++ b/solution.py
@@ -37,13 +37,13 @@
     number = {at: n for n, (at, _, _) in enumerate(faces)}
     touch = np.zeros((FACES, FINE), np.float32)
     lap = np.zeros((FINE, FINE), np.float32)
-    mean = np.zeros((FINE, 128), np.float32)
-    put_mean = np.zeros((128, PATCH), np.float32)
+    mean = np.zeros((FINE, 256), np.float32)
+    put_mean = np.zeros((256, PATCH), np.float32)
     cells = [(x, y, z) for x in range(8) for y in range(8) for z in range(8)]
     for cell, at in enumerate(cells):
         lap[cell, cell] = -6.0
         inner = [c // 2 + 1 for c in at]
-        box = (inner[0] - 1) * 16 + (inner[1] - 1) * 4 + inner[2] - 1
+        box = 96 + (inner[0] - 1) * 16 + (inner[1] - 1) * 4 + inner[2] - 1
         mean[cell, box] = 0.125
         put_mean[box, patch(inner)] = 1.0
         for axis, stride in enumerate((64, 8, 1)):
@@ -62,7 +62,7 @@
     for n, (at, near, axis) in enumerate(faces):
         q = patch(at)
         ghosts[q, n] = 1.0
-        ghosts[PATCH + q, FACES + n] = 1.0
+        ghosts[PATCH + q, 96 + n] = 1.0
         fixes[q, q] = 1.0 - 1.5
         fixes[patch(near), q] = -1.0
         fixes[PATCH + q, q] = -0.5
@@ -72,7 +72,10 @@
             sides[n // 16 * 64 + rest[0] * 8 + rest[1], n] = 1.0
     late = (touch @ mean @ put_mean) - 0.5 * put_face
     late[64:] = 0.0
-    return (lap_pool, touch, mean, ghosts, fixes, put_face, put_mean, sides, late)
+    both = np.zeros((2 * FACES, 2 * FINE), np.float32)
+    both[:96, :FINE] = touch[:96]
+    both[96:192, FINE:] = touch[:96]
+    return (lap_pool, both, mean, ghosts, fixes, put_face, put_mean, sides, late)
 
 
 def iota(shape, dim):
@@ -96,14 +99,26 @@
     return high, (value - high.astype(F32)).astype(BF)
 
 
-def fold(value):
-    half = value.shape[1] // 2
-    return jnp.concatenate([value[:, :half], value[:, half:]], axis=0)
-
-
-def unfold(value):
+def fold(value, width):
+    tiles = [value[n : n + 8, 128 : 128 + width] for n in range(0, SP, 8)]
+    if width == 32:
+        tiles = [jnp.concatenate(tiles + [jnp.zeros((8, 32), F32)], axis=1)]
+    else:
+        tiles = [
+            jnp.concatenate(tiles[:2], axis=1),
+            jnp.concatenate([tiles[2], jnp.zeros((8, 64), F32)], axis=1),
+        ]
+    return jnp.concatenate([value[:, :128]] + tiles, axis=0)
+
+
+def unfold(value, width):
     value = value.astype(F32)
-    return jnp.concatenate([value[:SP], value[SP:]], axis=1)
+    if width == 32:
+        tiles = [value[SP:, n * 32 : (n + 1) * 32] for n in range(3)]
+    else:
+        tiles = [value[SP : SP + 8, :64], value[SP : SP + 8, 64:], value[SP + 8 :, :64]]
+    rest = jnp.concatenate([jnp.concatenate(tiles, axis=0), jnp.zeros((SP, 128 - width), F32)], axis=1)
+    return jnp.concatenate([value[:SP], rest], axis=1)
 
 
 def kernel(
@@ -111,21 +126,28 @@
     n_yz,
     coarse,
     fine,
-    diffusion,
-    rate,
-    box_pos,
-    box_owner,
+    diffusion_in,
+    rate_in,
+    box_pos_in,
+    box_owner_in,
     lap_pool_in,
     touch_in,
     mean_in,
     ghosts_in,
     fixes_in,
-    put_face_in,
-    put_mean_in,
     sides_in,
     late_in,
-    coarse_out,
-    fine_out,
+    adv_out,
+    x_out,
+    y_out,
+    delta_out,
+    field_out,
+    back_in,
+    late_got,
+    diffusion,
+    rate,
+    box_pos,
+    box_owner,
     cv,
     fv,
     lap_pool,
@@ -133,8 +155,6 @@
     mean,
     ghosts,
     fixes,
-    put_face,
-    put_mean,
     sides,
     late,
     rz,
@@ -147,10 +167,10 @@
     ghost_out,
     ghost_in,
     back_out,
-    back_in,
     late_out,
-    late_got,
-    ov,
+    delta_tmp,
+    field_tmp,
+    plane_sem,
     load_sem,
     own_sem,
     halo_send,
@@ -177,19 +197,26 @@
         )
     pl.semaphore_signal(barrier, inc=1, device_id=(left, me), device_id_type=mesh_id)
 
+    planes = [pltpu.make_async_copy(coarse.at[x], cv.at[x], plane_sem.at[x]) for x in range(6)]
+    small = [
+        (rate_in, rate),
+        (diffusion_in, diffusion),
+        (box_pos_in, box_pos),
+        (box_owner_in, box_owner),
+    ]
+    small = [pltpu.make_async_copy(p[0], p[1], plane_sem.at[6 + n]) for n, p in enumerate(small)]
+    for copy in [planes[5]] + small + planes[:5]:
+        copy.start()
     loads = [
         pltpu.make_async_copy(src, dst, load_sem.at[n])
         for n, (src, dst) in enumerate(
             [
-                (coarse, cv),
                 (fine, fv),
                 (lap_pool_in, lap_pool),
                 (touch_in, touch),
                 (mean_in, mean),
                 (ghosts_in, ghosts),
                 (fixes_in, fixes),
-                (put_face_in, put_face),
-                (put_mean_in, put_mean),
                 (sides_in, sides),
                 (late_in, late),
             ]
@@ -218,29 +245,37 @@
         own.start()
         return copies, own
 
-    loads[0].wait()
-    for x in range(6):
+    def slab(x):
+        planes[x].wait()
         value = jnp.concatenate([cv[x], jnp.zeros((6, SP - S, NZ), F32)], axis=1)
         value = value.reshape(ROWS, NZ)
         xf[x] = value
         xh[x] = value.astype(BF)
-        if x % 2:
-            before = xf[x - 1]
-            first = jnp.concatenate([before[:SP], value[:SP]], axis=0)
-            last = jnp.concatenate([before[ROWS - SP :], value[ROWS - SP :]], axis=0)
-            ysend[0, x // 2] = first.astype(BF)
-            ysend[1, x // 2] = last.astype(BF)
-
-    pl.semaphore_wait(barrier, n_yz)
-    pl.semaphore_signal(ready, inc=1, device_id=(right, me), device_id_type=mesh_id)
+
     to_right = remote(xh.at[5], xrecv.at[0], halo_send, halo_recv, 0, (right, me))
     to_left = remote(xh.at[0], xrecv.at[1], halo_send, halo_recv, 1, (left, me))
     to_down = remote(ysend.at[0], yrecv.at[1], halo_send, halo_recv, 2, (gx, down))
     to_up = remote(ysend.at[1], yrecv.at[0], halo_send, halo_recv, 3, (gx, up))
+    slab(5)
+    pl.semaphore_wait(barrier, n_yz)
     to_right.start()
+    pl.semaphore_signal(ready, inc=1, device_id=(right, me), device_id_type=mesh_id)
+    for x in range(5):
+        slab(x)
+    for pair in range(3):
+        for side, part in ((0, slice(0, SP)), (1, slice(ROWS - SP, ROWS))):
+            layers = [xf[2 * pair, part], xf[2 * pair + 1, part]]
+            ysend[side, pair] = jnp.concatenate(layers, axis=0).astype(BF)
     to_down.start()
     to_up.start()
 
+    @pl.when(gx > 1)
+    def _():
+        pl.semaphore_wait(ready, 1)
+        to_left.start()
+
+    for copy in small:
+        copy.wait()
     rz[...] = jnp.zeros_like(rz)
     rz[0:S, 0:S] = rate[...]
     rate_high, rate_low = split(rz[...])
@@ -256,7 +291,8 @@
         full = dot_nt(dot(tall, part).astype(BF), tall)
         return jnp.where(y_row == y_col, full, 0.0).astype(BF)
 
-    mix_high, mix_low = mix(rate_high), mix(rate_low)
+    mix_high = mix(rate_high)
+    mix_both = jnp.concatenate([mix_high, mix(rate_low)], axis=0)
     at = iota((SP, 1), 0)
     column = jnp.zeros((SP, 1), F32)
     for s in range(S):
@@ -275,12 +311,15 @@
     take = one(iota((NZ, 256), 0) == want)
     y_lane = (iota((1, 256), 1) >> 3) & 7
 
-    def to_patch(slab):
-        cells = dot(slab, take)
-        patch = jnp.zeros((SP, 256), F32)
-        for y in range(6):
-            patch = jnp.where(y_lane == y, cells[y * SP : (y + 1) * SP], patch)
-        return patch
+    def to_patches(slabs):
+        cells = dot(jnp.concatenate(slabs, axis=0), take)
+        patches = []
+        for n in range(0, ROWS * len(slabs), ROWS):
+            patch = jnp.zeros((SP, 256), F32)
+            for y in range(6):
+                patch = jnp.where(y_lane == y, cells[n + y * SP : n + (y + 1) * SP], patch)
+            patches.append(patch)
+        return patches
 
     def by_box(parts):
         rows = [
@@ -296,7 +335,13 @@
             total = total + jnp.where(sent, value[i * SP : (i + 1) * SP], 0.0)
         return total
 
-    olds, news = [], []
+    stores = []
+
+    def put(src, dst, n):
+        stores.append(pltpu.make_async_copy(src, dst, out_sem.at[n]))
+        stores[-1].start()
+
+    news = []
     for x in range(6):
         value = xf[x]
         high = xh[x]
@@ -309,22 +354,24 @@
         rest = jnp.zeros((SP, NZ), F32)
         around = around + jnp.concatenate([rest, value[: ROWS - SP]], axis=0)
         around = around + jnp.concatenate([value[SP:], rest], axis=0)
-        mixed = dot(mix_high, high) + dot(mix_low, high) + dot(mix_high, low)
+        mixed = dot(mix_both, high)
+        mixed = mixed[:ROWS] + mixed[ROWS:] + dot(mix_high, low)
         value = value + mixed + d_slab * around
         adv[x] = value
-        olds.append(to_patch(high))
-        news.append(to_patch(value.astype(BF)))
-    patches = jnp.concatenate([by_box(olds), by_box(news)], axis=1).astype(BF)
-    for n in (5, 6):
+        put(adv.at[x], adv_out.at[x], x)
+        news.append(value.astype(BF))
+    olds = by_box(to_patches([xh[x] for x in range(6)]))
+    patches = jnp.concatenate([olds, by_box(to_patches(news))], axis=1).astype(BF)
+    for n in (4, 5):
         loads[n].wait()
     sent = dot(patches, ghosts[...])
     flag = jnp.concatenate([one(at == FLAG, F32)] * 4, axis=0)
     sent = sent + flag
     for owner in range(8):
-        ghost_out[owner] = fold(for_owner(sent, owner)).astype(BF)
+        ghost_out[owner] = fold(for_owner(sent, owner), 64).astype(BF)
     ghost_copies, own_ghost = exchange(ghost_out, ghost_in, ghost_send, ghost_recv, 0)
 
-    for n in (1, 2, 3, 4):
+    for n in (0, 1, 2, 3):
         loads[n].wait()
     field = fv[...].astype(F32).reshape(S * 8, FINE)
     field = jnp.concatenate([field, jnp.zeros((8, FINE), F32)], axis=0)
@@ -335,7 +382,8 @@
         full = dot_nt(dot(tall, part).astype(BF), tall)
         return jnp.where(slot_same, 0.5 * full, 0.0).astype(BF)
 
-    slot_high, slot_low = slot_rate(rate_high), slot_rate(rate_low)
+    slot_high = slot_rate(rate_high)
+    slot_both = jnp.concatenate([slot_high, slot_rate(rate_low)], axis=0)
     d_slot = [jnp.full((8, 1), diffusion[s], F32) for s in range(S)]
     d_slot = jnp.concatenate(d_slot + [jnp.zeros((8, 1), F32)], axis=0)
     row = iota((SLOT, 8 * SP), 0)
@@ -345,49 +393,63 @@
     outward = one(outward, F32).reshape(8 * SP, SLOT).astype(BF)
     high = field.astype(BF)
     both = dot(high, lap_pool[...])
+    mixed = dot(slot_both, high)
     pooled = both[:, FINE:]
     field = (
-        field + (2.0 * d_slot) * both[:, :FINE] + (dot(slot_high, high) + dot(slot_low, high))
+        field + (2.0 * d_slot) * both[:, :FINE] + mixed[:SLOT] + mixed[SLOT:]
     )
 
     for copy in ghost_copies:
         copy.wait_recv()
     own_ghost.wait()
-    pl.semaphore_wait(ready, 1)
-    to_left.start()
-
-    got = jnp.concatenate([unfold(ghost_in[j]) for j in range(8)], axis=0).astype(BF)
+
+    got = jnp.concatenate([unfold(ghost_in[j], 64) for j in range(8)], axis=0).astype(BF)
     got = dot(inward, got)
     used = jnp.concatenate([got[S * 8 :, 0:1]] * (SLOT // 8), axis=0) > 0.5
     got = got.astype(BF)
-    ghost_old = dot(got[:, :FACES], touch[...])
-    ghost_mid = 0.5 * (ghost_old + dot(got[:, FACES:], touch[...]))
+    spread = dot(got, touch[...])
+    ghost_old = spread[:, :FINE]
+    ghost_mid = 0.5 * (ghost_old + spread[:, FINE:])
     field = field + (2.0 * d_slot) * ghost_old
     high, low = split(field)
-    both = dot(high, lap_pool[...]) + dot(low, lap_pool[...])
+    both = dot(jnp.concatenate([high, low], axis=0), lap_pool[...])
+    both = both[:SLOT] + both[SLOT:]
+    mixed = dot(slot_both, high)
     pooled = pooled + both[:, FINE:]
     field = (
         field
         + (2.0 * d_slot) * (both[:, :FINE] + ghost_mid)
-        + (dot(slot_high, high) + dot(slot_low, high) + dot(slot_high, low))
+        + (mixed[:SLOT] + mixed[SLOT:] + dot(slot_high, low))
     )
-    back = jnp.concatenate([pooled, dot(field.astype(BF), mean[...])], axis=1)
+    field_tmp[...] = jnp.where(used, field, 0.0)
+    back = dot(field.astype(BF), mean[...])
+    back = jnp.concatenate([back[:, :FACES] + pooled, back[:, FACES:]], axis=1)
     back = dot(outward, back.astype(BF))
     for host in range(8):
-        back_out[host] = fold(back[host * SP : (host + 1) * SP]).astype(BF)
+        back_out[host] = fold(back[host * SP : (host + 1) * SP], 32).astype(BF)
     back_copies, own_back = exchange(back_out, back_in, back_send, back_recv, 1)
 
-    for n in (7, 8, 9, 10):
+    put(field_tmp, field_out, 6)
+
+    @pl.when(gx <= 1)
+    def _():
+        pl.semaphore_wait(ready, 1)
+        to_left.start()
+
+    for n in (6, 7):
         loads[n].wait()
-    for copy in (to_down, to_up, to_left, to_right):
-        copy.wait_recv()
-    layers = [
-        xrecv[0],
-        xrecv[1],
-        jnp.concatenate([yrecv[0, pair] for pair in range(3)], axis=0),
-        jnp.concatenate([yrecv[1, pair] for pair in range(3)], axis=0),
-    ]
-    added = by_box([to_patch(layer) for layer in layers]).astype(BF)
+    delta = dot(patches, fixes[...])
+    to_down.wait_recv()
+    to_up.wait_recv()
+    put(yrecv, y_out, 7)
+    layers = [jnp.concatenate([yrecv[n, pair] for pair in range(3)], axis=0) for n in range(2)]
+    to_left.wait_recv()
+    put(xrecv.at[1], x_out.at[1], 8)
+    parts = to_patches([xrecv[1]] + layers)
+    to_right.wait_recv()
+    put(xrecv.at[0], x_out.at[0], 9)
+    parts = to_patches([xrecv[0]]) + parts
+    added = by_box(parts).astype(BF)
     added = dot(added, sides[...])
     for owner in range(8):
         part = for_owner(added, owner)
@@ -396,38 +458,122 @@
         late_out[owner] = jnp.concatenate([first, last], axis=0).astype(BF)
     late_copies, own_late = exchange(late_out, late_got, late_send, late_recv, 2)
 
+    delta_tmp[...] = d_box * (delta + d_box * dot(added.astype(BF), late[...]))
+    put(delta_tmp, delta_out, 10)
+
+    for copy in [to_right, to_left, to_down, to_up] + ghost_copies:
+        copy.wait_send()
+    for copy in back_copies + late_copies:
+        copy.wait()
+    own_back.wait()
+    own_late.wait()
+    for copy in stores:
+        copy.wait()
+
+
+def finish(
+    adv_in,
+    x_in,
+    y_in,
+    delta_in,
+    field_in,
+    back_in,
+    late_in,
+    touch_in,
+    put_face_in,
+    put_mean_in,
+    diffusion_in,
+    box_pos_in,
+    box_owner_in,
+    coarse_out,
+    fine_out,
+    diffusion,
+    box_pos,
+    box_owner,
+    adv,
+    x_halo,
+    y_halo,
+    delta_part,
+    field,
+    back,
+    late_got,
+    touch,
+    put_face,
+    put_mean,
+    ov,
+    fv,
+    load_sem,
+    out_sem,
+):
+    pairs = [
+        (back_in, back),
+        (put_face_in, put_face),
+        (put_mean_in, put_mean),
+        (delta_in, delta_part),
+        (x_in, x_halo),
+        (y_in, y_halo),
+        (late_in, late_got),
+        (touch_in, touch),
+        (field_in, field),
+    ]
+    pairs += [(adv_in.at[x], adv.at[x]) for x in range(6)]
+    loads = [pltpu.make_async_copy(p[0], p[1], load_sem.at[n]) for n, p in enumerate(pairs)]
+    small = [(box_pos_in, box_pos), (box_owner_in, box_owner), (diffusion_in, diffusion)]
+    small = [pltpu.make_async_copy(p[0], p[1], load_sem.at[15 + n]) for n, p in enumerate(small)]
+    for copy in small + loads:
+        copy.start()
+    for copy in small:
+        copy.wait()
+
+    at = iota((SP, 1), 0)
+    column = jnp.zeros((SP, 1), F32)
+    for s in range(S):
+        column = jnp.where(at == s, diffusion[s], column)
+    d_slab = jnp.concatenate([column] * 6, axis=0)
+    d_box = jnp.concatenate([column] * 4, axis=0)
+    d_slot = [jnp.full((8, 1), diffusion[s], F32) for s in range(S)]
+    d_slot = jnp.concatenate(d_slot + [jnp.zeros((8, 1), F32)], axis=0)
+    row = iota((SLOT, 8 * SP), 0)
+    inward = one(iota((SLOT, 8 * SP), 1) == (row & 7) * SP + (row >> 3))
     lane = iota((256, 1), 0)
-    want = jnp.where((lane & 7) < 6, start_of(lane >> 6) + (lane & 7), -1)
-    give = one(iota((256, NZ), 1) == want)
-    delta = dot(patches, fixes[...])
-    delta = delta + d_box * dot(added.astype(BF), late[...])
-    for copy in back_copies:
-        copy.wait_recv()
-    own_back.wait()
-    mine = [unfold(back_in[box_owner[0, 0, i]]) for i in range(4)]
-    mine = jnp.concatenate(mine, axis=0).astype(BF)
-    delta = d_box * (delta + dot(mine[:, :FACES], put_face[...]))
-    delta = delta + dot(mine[:, FACES:], put_mean[...])
+    place = jnp.full((256, 1), box_pos[0, 0, 0] * 6, jnp.int32)
+    for i in range(1, 4):
+        place = jnp.where((lane >> 6) == i, box_pos[0, 0, i] * 6, place)
+    give = one(iota((256, NZ), 1) == jnp.where((lane & 7) < 6, place + (lane & 7), -1))
+    y_lane = (iota((1, 256), 1) >> 3) & 7
     zat = iota((1, NZ), 1)
     inside = jnp.zeros((1, NZ), jnp.int32)
     for i in range(4):
         offset = zat - box_pos[0, 0, i] * 6
         inside = inside + jnp.where((offset >= 1) & (offset <= 4), 1, 0)
+
+    for copy in loads[:4]:
+        copy.wait()
+    mine = [unfold(back[box_owner[0, 0, i]], 32) for i in range(4)]
+    mine = jnp.concatenate(mine, axis=0).astype(BF)
+    delta = delta_part[...] + d_box * dot(mine[:, :FACES], put_face[...])
+    delta = delta + dot(mine, put_mean[...])
+    cells = []
+    for x in range(6):
+        part = [delta[i * SP : (i + 1) * SP, x * 64 : (x + 1) * 64] for i in range(4)]
+        part = jnp.concatenate(part, axis=1)
+        cells += [jnp.where(y_lane == y, part, 0.0) for y in range(6)]
+    changes = dot(jnp.concatenate(cells, axis=0).astype(BF), give)
+    for copy in loads[4:6]:
+        copy.wait()
     stores = []
     rest = jnp.zeros((ROWS - 2 * SP, NZ), F32)
     for x in range(6):
+        loads[9 + x].wait()
         part = slice((x % 2) * SP, (x % 2 + 1) * SP)
-        before = yrecv[0, x // 2].astype(F32)[part]
-        after = yrecv[1, x // 2].astype(F32)[part]
+        before = y_halo[0, x // 2].astype(F32)[part]
+        after = y_halo[1, x // 2].astype(F32)[part]
         around = jnp.concatenate([before, rest, after], axis=0)
         if x == 0:
-            around = around + xrecv[0].astype(F32)
+            around = around + x_halo[0].astype(F32)
         if x == 5:
-            around = around + xrecv[1].astype(F32)
-        part = [delta[i * SP : (i + 1) * SP, x * 64 : (x + 1) * 64] for i in range(4)]
-        part = jnp.concatenate(part, axis=1)
-        cells = [jnp.where(y_lane == y, part, 0.0) for y in range(6)]
-        change = dot(jnp.concatenate(cells, axis=0).astype(BF), give)
+            around = around + x_halo[1].astype(F32)
+        change = changes[x * ROWS : (x + 1) * ROWS]
         total = adv[x] + d_slab * around + change
         if 1 <= x <= 4:
             middle = jnp.where(inside > 0, change[SP : ROWS - SP], total[SP : ROWS - SP])
@@ -436,41 +582,47 @@
         stores.append(pltpu.make_async_copy(ov.at[x], coarse_out.at[x], out_sem.at[x]))
         stores[-1].start()
 
-    for copy in late_copies:
-        copy.wait_recv()
-    own_late.wait()
+    for copy in loads[6:9]:
+        copy.wait()
     parts = []
     for j in range(8):
         value = late_got[j].astype(F32)
         parts += [value[:8, :64], value[:8, 64:], value[8:, :64]]
     got = dot(inward, jnp.concatenate(parts, axis=0).astype(BF)).astype(BF)
-    field = field + (d_slot * d_slot) * dot(got, touch[0:64])
-    field = jnp.where(used, field, 0.0)
-    fine_out[...] = field[: S * 8].reshape(S, 8, FINE).astype(BF)
-
-    for copy in [to_right, to_left, to_down, to_up] + ghost_copies + back_copies + late_copies:
-        copy.wait_send()
+    total = field[...] + (d_slot * d_slot) * dot(got, touch[...])
+    fv[...] = total[: S * 8].reshape(S, 8, FINE).astype(BF)
+    stores.append(pltpu.make_async_copy(fv, fine_out, out_sem.at[6]))
+    stores[-1].start()
     for copy in stores:
         copy.wait()
 
 
 def local(n_gx, n_yz, consts, coarse_state, fine_state, diffusion, rate, box_pos, box_owner):
     hbm = pl.BlockSpec(memory_space=pl.ANY)
-    vmem = pl.BlockSpec(memory_space=pltpu.VMEM)
-    smem = pl.BlockSpec(memory_space=pltpu.SMEM)
     dma = pltpu.SemaphoreType.DMA
-    coarse, fine = pl.pallas_call(
+    first = [consts[n] for n in (0, 1, 2, 3, 4, 7, 8)]
+    middle = [
+        ((6, ROWS, NZ), F32),
+        ((2, ROWS, NZ), BF),
+        ((2, 3, 2 * SP, NZ), BF),
+        ((4 * SP, PATCH), F32),
+        ((SLOT, FINE), F32),
+        ((8, 32, 128), BF),
+        ((8, 16, 128), BF),
+    ]
+    between = pl.pallas_call(
         functools.partial(kernel, n_gx, n_yz),
-        out_shape=(
-            jax.ShapeDtypeStruct((6, 6, S, NZ), F32),
-            jax.ShapeDtypeStruct((S, 8, FINE), BF),
-        ),
-        in_specs=[hbm, hbm, smem, vmem, smem, smem] + [hbm] * len(consts),
-        out_specs=(hbm, vmem),
+        out_shape=tuple(jax.ShapeDtypeStruct(*m) for m in middle),
+        in_specs=[hbm] * (6 + len(first)),
+        out_specs=(hbm,) * len(middle),
         scratch_shapes=[
+            pltpu.SMEM((S,), F32),
+            pltpu.VMEM((S, S), F32),
+            pltpu.SMEM((1, 1, 4), jnp.int32),
+            pltpu.SMEM((1, 1, 4), jnp.int32),
             pltpu.VMEM((6, 6, S, NZ), F32),
             pltpu.VMEM((S, 8, FINE), BF),
-            *[pltpu.VMEM(c.shape, BF) for c in consts],
+            *[pltpu.VMEM(c.shape, BF) for c in first],
             pltpu.VMEM((128, 128), F32),
             pltpu.VMEM((6, ROWS, NZ), F32),
             pltpu.VMEM((6, ROWS, NZ), BF),
@@ -478,15 +630,18 @@
             pltpu.VMEM((2, 3, 2 * SP, NZ), BF),
             pltpu.VMEM((2, 3, 2 * SP, NZ), BF),
             pltpu.VMEM((2, ROWS, NZ), BF),
-            *[pltpu.VMEM((8, 2 * SP, 128), BF)] * 4,
-            *[pltpu.VMEM((8, 16, 128), BF)] * 2,
-            pltpu.VMEM((6, 6, S, NZ), F32),
-            dma((2 + len(consts),)),
+            *[pltpu.VMEM((8, 40, 128), BF)] * 2,
+            pltpu.VMEM((8, 32, 128), BF),
+            pltpu.VMEM((8, 16, 128), BF),
+            pltpu.VMEM((4 * SP, PATCH), F32),
+            pltpu.VMEM((SLOT, FINE), F32),
+            dma((10,)),
+            dma((1 + len(first),)),
             dma((3,)),
             dma((4,)),
             dma((4,)),
             *[dma((8,))] * 6,
-            dma((6,)),
+            dma((11,)),
             pltpu.SemaphoreType.REGULAR,
         ],
         compiler_params=pltpu.CompilerParams(
@@ -500,8 +655,31 @@
         rate,
         box_pos,
         box_owner,
-        *consts,
+        *first,
     )
+    last = [consts[1][:64, :FINE], consts[5], consts[6]]
+    coarse, fine = pl.pallas_call(
+        finish,
+        out_shape=(
+            jax.ShapeDtypeStruct((6, 6, S, NZ), F32),
+            jax.ShapeDtypeStruct((S, 8, FINE), BF),
+        ),
+        in_specs=[hbm] * (len(middle) + len(last) + 3),
+        out_specs=(hbm, hbm),
+        scratch_shapes=[
+            pltpu.SMEM((S,), F32),
+            pltpu.SMEM((1, 1, 4), jnp.int32),
+            pltpu.SMEM((1, 1, 4), jnp.int32),
+            *[pltpu.VMEM(*m) for m in middle],
+            *[pltpu.VMEM(c.shape, BF) for c in last],
+            pltpu.VMEM((6, 6, S, NZ), F32),
+            pltpu.VMEM((S, 8, FINE), BF),
+            dma((18,)),
+            dma((7,)),
+        ],
+        compiler_params=pltpu.CompilerParams(vmem_limit_bytes=56 * 1024 * 1024),
+        name="finish",
+    )(*between, *last, diffusion, box_pos, box_owner)
     return jnp.transpose(coarse, (2, 0, 1, 3)), jnp.transpose(fine, (1, 0, 2))
 
 

time: 32.8 us -> 30.9 us (0.942)
  local copies, waits for them, and re-layouts: 3.18 us -> 0 us
  Pallas kernels: 28.8 us -> 30 us
    unnamed x4 -> x0, local copies, waits for them, and re-layouts: 3.18 us -> none
    pallas_call x1 -> x2, Pallas kernels: 28.8 us -> 30 us  [the longest x1 26.8 us: local(): pl.pallas_call(functools.partial(kernel, n_gx, n_yz), out_shape=tuple((ja...]
where the time goes in v2:
time: 30.9 us; the launch traced here: 30.7 us
  Pallas kernels  30 us (97%)
  between operations  0.64 us (2%)
    pallas_call x1, Pallas kernels, local(): pl.pallas_call(functools.partial(kernel, n_gx, n_yz), out_shape=tuple((ja...  26.8 us
    pallas_call x1, Pallas kernels, local(): pl.pallas_call(finish, out_shape=(jax.ShapeDtypeStruct((6, 6, S, NZ), F32...  3.23 us

profile of v2, /device:TPU:8, one launch (start us, length us, event | category | flops | bytes accessed | tf_op | source)
XLA Modules:
  0.0 30.7 jit_solution(16862565774636833792)
XLA Ops:
  0.6 26.8 %amr_step.1 = (f32[6,144,384]{2,1,0:T(8,128)}, bf16[2,144,384]{2,1,0:T(8,128)(2,1)}, bf16[2,3,48,384]{3,2,1,0:T(8,128)(2,1)}, f32[96,384]{1,0:T(8,128)}, f32[176...) custom-call(f32[6,6,21,384]{3,2,1,0:T(8,128)} %bitcast.4, bf16[21,8,512]{2,1,0:T(8,128)(2,1)} %bitcast.5, ...), custom_call_target="tpu_custom_call" | custom-call | tf_op jit(solution)/shard_map/amr_step/pallas_call | solution.py:613
  27.4 3.2 %finish.1 = (f32[6,6,21,384]{3,2,1,0:T(8,128)}, bf16[21,8,512]{2,1,0:T(8,128)(2,1)}) custom-call(f32[6,144,384]{2,1,0:T(8,128)} %get-tuple-element.11.adv_in, bf16[2,144,384]{2,1,0:T(8,128)(2,1)} %get-tuple-element.12.x_in, bf16[2,3,48,384]{3,2,1,0:T(8,128)(2,1)} %get-tuple-element.13.y_in, f32[96,384]{1,0:T(8,128)} %get-tuple-element.14.delta_in, ...), custom_call_target="tpu_custom_call" | custom-call | tf_op jit(solution)/shard_map/finish/pallas_call | solution.py:661

commit v3 on v2

--- a/solution.py
+++ b/solution.py
@@ -135,14 +135,12 @@
     mean_in,
     ghosts_in,
     fixes_in,
+    put_face_in,
+    put_mean_in,
     sides_in,
     late_in,
-    adv_out,
-    x_out,
-    y_out,
-    delta_out,
+    coarse_mid,
     field_out,
-    back_in,
     late_got,
     diffusion,
     rate,
@@ -155,6 +153,8 @@
     mean,
     ghosts,
     fixes,
+    put_face,
+    put_mean,
     sides,
     late,
     rz,
@@ -167,9 +167,10 @@
     ghost_out,
     ghost_in,
     back_out,
+    back_in,
     late_out,
-    delta_tmp,
     field_tmp,
+    ov,
     plane_sem,
     load_sem,
     own_sem,
@@ -190,6 +191,9 @@
     up, down = lax.rem(me + 1, n_yz), lax.rem(me + n_yz - 1, n_yz)
     mesh_id = pl.DeviceIdType.MESH
 
+    planes = [pltpu.make_async_copy(coarse.at[x], cv.at[x], plane_sem.at[x]) for x in range(6)]
+    planes[5].start()
+
     barrier = pltpu.get_barrier_semaphore()
     for step in range(1, n_yz):
         pl.semaphore_signal(
@@ -197,7 +201,6 @@
         )
     pl.semaphore_signal(barrier, inc=1, device_id=(left, me), device_id_type=mesh_id)
 
-    planes = [pltpu.make_async_copy(coarse.at[x], cv.at[x], plane_sem.at[x]) for x in range(6)]
     small = [
         (rate_in, rate),
         (diffusion_in, diffusion),
@@ -205,7 +208,7 @@
         (box_owner_in, box_owner),
     ]
     small = [pltpu.make_async_copy(p[0], p[1], plane_sem.at[6 + n]) for n, p in enumerate(small)]
-    for copy in [planes[5]] + small + planes[:5]:
+    for copy in small + planes[:5]:
         copy.start()
     loads = [
         pltpu.make_async_copy(src, dst, load_sem.at[n])
@@ -217,6 +220,8 @@
                 (mean_in, mean),
                 (ghosts_in, ghosts),
                 (fixes_in, fixes),
+                (put_face_in, put_face),
+                (put_mean_in, put_mean),
                 (sides_in, sides),
                 (late_in, late),
             ]
@@ -358,7 +363,6 @@
         mixed = mixed[:ROWS] + mixed[ROWS:] + dot(mix_high, low)
         value = value + mixed + d_slab * around
         adv[x] = value
-        put(adv.at[x], adv_out.at[x], x)
         news.append(value.astype(BF))
     olds = by_box(to_patches([xh[x] for x in range(6)]))
     patches = jnp.concatenate([olds, by_box(to_patches(news))], axis=1).astype(BF)
@@ -431,23 +435,29 @@
 
     put(field_tmp, field_out, 6)
 
+    lane = iota((256, 1), 0)
+    want = jnp.where((lane & 7) < 6, start_of(lane >> 6) + (lane & 7), -1)
+    give = one(iota((256, NZ), 1) == want)
+    zat = iota((1, NZ), 1)
+    inside = jnp.zeros((1, NZ), jnp.int32)
+    for i in range(4):
+        offset = zat - box_pos[0, 0, i] * 6
+        inside = inside + jnp.where((offset >= 1) & (offset <= 4), 1, 0)
+
     @pl.when(gx <= 1)
     def _():
         pl.semaphore_wait(ready, 1)
         to_left.start()
 
-    for n in (6, 7):
+    for n in (6, 7, 8, 9):
         loads[n].wait()
     delta = dot(patches, fixes[...])
     to_down.wait_recv()
     to_up.wait_recv()
-    put(yrecv, y_out, 7)
     layers = [jnp.concatenate([yrecv[n, pair] for pair in range(3)], axis=0) for n in range(2)]
     to_left.wait_recv()
-    put(xrecv.at[1], x_out.at[1], 8)
     parts = to_patches([xrecv[1]] + layers)
     to_right.wait_recv()
-    put(xrecv.at[0], x_out.at[0], 9)
     parts = to_patches([xrecv[0]]) + parts
     added = by_box(parts).astype(BF)
     added = dot(added, sides[...])
@@ -458,100 +468,13 @@
         late_out[owner] = jnp.concatenate([first, last], axis=0).astype(BF)
     late_copies, own_late = exchange(late_out, late_got, late_send, late_recv, 2)
 
-    delta_tmp[...] = d_box * (delta + d_box * dot(added.astype(BF), late[...]))
-    put(delta_tmp, delta_out, 10)
-
-    for copy in [to_right, to_left, to_down, to_up] + ghost_copies:
-        copy.wait_send()
-    for copy in back_copies + late_copies:
-        copy.wait()
+    delta = d_box * (delta + d_box * dot(added.astype(BF), late[...]))
+    for copy in back_copies:
+        copy.wait_recv()
     own_back.wait()
-    own_late.wait()
-    for copy in stores:
-        copy.wait()
-
-
-def finish(
-    adv_in,
-    x_in,
-    y_in,
-    delta_in,
-    field_in,
-    back_in,
-    late_in,
-    touch_in,
-    put_face_in,
-    put_mean_in,
-    diffusion_in,
-    box_pos_in,
-    box_owner_in,
-    coarse_out,
-    fine_out,
-    diffusion,
-    box_pos,
-    box_owner,
-    adv,
-    x_halo,
-    y_halo,
-    delta_part,
-    field,
-    back,
-    late_got,
-    touch,
-    put_face,
-    put_mean,
-    ov,
-    fv,
-    load_sem,
-    out_sem,
-):
-    pairs = [
-        (back_in, back),
-        (put_face_in, put_face),
-        (put_mean_in, put_mean),
-        (delta_in, delta_part),
-        (x_in, x_halo),
-        (y_in, y_halo),
-        (late_in, late_got),
-        (touch_in, touch),
-        (field_in, field),
-    ]
-    pairs += [(adv_in.at[x], adv.at[x]) for x in range(6)]
-    loads = [pltpu.make_async_copy(p[0], p[1], load_sem.at[n]) for n, p in enumerate(pairs)]
-    small = [(box_pos_in, box_pos), (box_owner_in, box_owner), (diffusion_in, diffusion)]
-    small = [pltpu.make_async_copy(p[0], p[1], load_sem.at[15 + n]) for n, p in enumerate(small)]
-    for copy in small + loads:
-        copy.start()
-    for copy in small:
-        copy.wait()
-
-    at = iota((SP, 1), 0)
-    column = jnp.zeros((SP, 1), F32)
-    for s in range(S):
-        column = jnp.where(at == s, diffusion[s], column)
-    d_slab = jnp.concatenate([column] * 6, axis=0)
-    d_box = jnp.concatenate([column] * 4, axis=0)
-    d_slot = [jnp.full((8, 1), diffusion[s], F32) for s in range(S)]
-    d_slot = jnp.concatenate(d_slot + [jnp.zeros((8, 1), F32)], axis=0)
-    row = iota((SLOT, 8 * SP), 0)
-    inward = one(iota((SLOT, 8 * SP), 1) == (row & 7) * SP + (row >> 3))
-    lane = iota((256, 1), 0)
-    place = jnp.full((256, 1), box_pos[0, 0, 0] * 6, jnp.int32)
-    for i in range(1, 4):
-        place = jnp.where((lane >> 6) == i, box_pos[0, 0, i] * 6, place)
-    give = one(iota((256, NZ), 1) == jnp.where((lane & 7) < 6, place + (lane & 7), -1))
-    y_lane = (iota((1, 256), 1) >> 3) & 7
-    zat = iota((1, NZ), 1)
-    inside = jnp.zeros((1, NZ), jnp.int32)
-    for i in range(4):
-        offset = zat - box_pos[0, 0, i] * 6
-        inside = inside + jnp.where((offset >= 1) & (offset <= 4), 1, 0)
-
-    for copy in loads[:4]:
-        copy.wait()
-    mine = [unfold(back[box_owner[0, 0, i]], 32) for i in range(4)]
+    mine = [unfold(back_in[box_owner[0, 0, i]], 32) for i in range(4)]
     mine = jnp.concatenate(mine, axis=0).astype(BF)
-    delta = delta_part[...] + d_box * dot(mine[:, :FACES], put_face[...])
+    delta = delta + d_box * dot(mine[:, :FACES], put_face[...])
     delta = delta + dot(mine, put_mean[...])
     cells = []
     for x in range(6):
@@ -559,30 +482,70 @@
         part = jnp.concatenate(part, axis=1)
         cells += [jnp.where(y_lane == y, part, 0.0) for y in range(6)]
     changes = dot(jnp.concatenate(cells, axis=0).astype(BF), give)
-    for copy in loads[4:6]:
-        copy.wait()
-    stores = []
     rest = jnp.zeros((ROWS - 2 * SP, NZ), F32)
     for x in range(6):
-        loads[9 + x].wait()
         part = slice((x % 2) * SP, (x % 2 + 1) * SP)
-        before = y_halo[0, x // 2].astype(F32)[part]
-        after = y_halo[1, x // 2].astype(F32)[part]
+        before = yrecv[0, x // 2].astype(F32)[part]
+        after = yrecv[1, x // 2].astype(F32)[part]
         around = jnp.concatenate([before, rest, after], axis=0)
         if x == 0:
-            around = around + x_halo[0].astype(F32)
+            around = around + xrecv[0].astype(F32)
         if x == 5:
-            around = around + x_halo[1].astype(F32)
+            around = around + xrecv[1].astype(F32)
         change = changes[x * ROWS : (x + 1) * ROWS]
         total = adv[x] + d_slab * around + change
         if 1 <= x <= 4:
             middle = jnp.where(inside > 0, change[SP : ROWS - SP], total[SP : ROWS - SP])
             total = jnp.concatenate([total[:SP], middle, total[ROWS - SP :]], axis=0)
         ov[x] = total.reshape(6, SP, NZ)[:, :S]
-        stores.append(pltpu.make_async_copy(ov.at[x], coarse_out.at[x], out_sem.at[x]))
+        put(ov.at[x], coarse_mid.at[x], x)
+
+    for copy in [to_right, to_left, to_down, to_up] + ghost_copies + back_copies:
+        copy.wait_send()
+    for copy in late_copies:
+        copy.wait()
+    own_late.wait()
+    for copy in stores:
+        copy.wait()
+
+
+def finish(
+    coarse_in,
+    field_in,
+    late_in,
+    touch_in,
+    diffusion_in,
+    coarse_out,
+    fine_out,
+    diffusion,
+    cells,
+    field,
+    late_got,
+    touch,
+    fv,
+    load_sem,
+    out_sem,
+):
+    pairs = [(late_in, late_got), (touch_in, touch), (field_in, field)]
+    pairs += [(coarse_in.at[x], cells.at[x]) for x in range(6)]
+    loads = [pltpu.make_async_copy(p[0], p[1], load_sem.at[n]) for n, p in enumerate(pairs)]
+    small = pltpu.make_async_copy(diffusion_in, diffusion, load_sem.at[9])
+    small.start()
+    for copy in loads:
+        copy.start()
+    small.wait()
+
+    d_slot = [jnp.full((8, 1), diffusion[s], F32) for s in range(S)]
+    d_slot = jnp.concatenate(d_slot + [jnp.zeros((8, 1), F32)], axis=0)
+    row = iota((SLOT, 8 * SP), 0)
+    inward = one(iota((SLOT, 8 * SP), 1) == (row & 7) * SP + (row >> 3))
+    stores = []
+    for x in range(6):
+        loads[3 + x].wait()
+        stores.append(pltpu.make_async_copy(cells.at[x], coarse_out.at[x], out_sem.at[x]))
         stores[-1].start()
 
-    for copy in loads[6:9]:
+    for copy in loads[:3]:
         copy.wait()
     parts = []
     for j in range(8):
@@ -600,20 +563,11 @@
 def local(n_gx, n_yz, consts, coarse_state, fine_state, diffusion, rate, box_pos, box_owner):
     hbm = pl.BlockSpec(memory_space=pl.ANY)
     dma = pltpu.SemaphoreType.DMA
-    first = [consts[n] for n in (0, 1, 2, 3, 4, 7, 8)]
-    middle = [
-        ((6, ROWS, NZ), F32),
-        ((2, ROWS, NZ), BF),
-        ((2, 3, 2 * SP, NZ), BF),
-        ((4 * SP, PATCH), F32),
-        ((SLOT, FINE), F32),
-        ((8, 32, 128), BF),
-        ((8, 16, 128), BF),
-    ]
+    middle = [((6, 6, S, NZ), F32), ((SLOT, FINE), F32), ((8, 16, 128), BF)]
     between = pl.pallas_call(
         functools.partial(kernel, n_gx, n_yz),
         out_shape=tuple(jax.ShapeDtypeStruct(*m) for m in middle),
-        in_specs=[hbm] * (6 + len(first)),
+        in_specs=[hbm] * (6 + len(consts)),
         out_specs=(hbm,) * len(middle),
         scratch_shapes=[
             pltpu.SMEM((S,), F32),
@@ -622,7 +576,7 @@
             pltpu.SMEM((1, 1, 4), jnp.int32),
             pltpu.VMEM((6, 6, S, NZ), F32),
             pltpu.VMEM((S, 8, FINE), BF),
-            *[pltpu.VMEM(c.shape, BF) for c in first],
+            *[pltpu.VMEM(c.shape, BF) for c in consts],
             pltpu.VMEM((128, 128), F32),
             pltpu.VMEM((6, ROWS, NZ), F32),
             pltpu.VMEM((6, ROWS, NZ), BF),
@@ -631,12 +585,12 @@
             pltpu.VMEM((2, 3, 2 * SP, NZ), BF),
             pltpu.VMEM((2, ROWS, NZ), BF),
             *[pltpu.VMEM((8, 40, 128), BF)] * 2,
-            pltpu.VMEM((8, 32, 128), BF),
+            *[pltpu.VMEM((8, 32, 128), BF)] * 2,
             pltpu.VMEM((8, 16, 128), BF),
-            pltpu.VMEM((4 * SP, PATCH), F32),
             pltpu.VMEM((SLOT, FINE), F32),
+            pltpu.VMEM((6, 6, S, NZ), F32),
             dma((10,)),
-            dma((1 + len(first),)),
+            dma((1 + len(consts),)),
             dma((3,)),
             dma((4,)),
             dma((4,)),
@@ -655,31 +609,28 @@
         rate,
         box_pos,
         box_owner,
-        *first,
+        *consts,
     )
-    last = [consts[1][:64, :FINE], consts[5], consts[6]]
+    last = consts[1][:64, :FINE]
     coarse, fine = pl.pallas_call(
         finish,
         out_shape=(
             jax.ShapeDtypeStruct((6, 6, S, NZ), F32),
             jax.ShapeDtypeStruct((S, 8, FINE), BF),
         ),
-        in_specs=[hbm] * (len(middle) + len(last) + 3),
+        in_specs=[hbm] * (len(middle) + 2),
         out_specs=(hbm, hbm),
         scratch_shapes=[
             pltpu.SMEM((S,), F32),
-            pltpu.SMEM((1, 1, 4), jnp.int32),
-            pltpu.SMEM((1, 1, 4), jnp.int32),
             *[pltpu.VMEM(*m) for m in middle],
-            *[pltpu.VMEM(c.shape, BF) for c in last],
-            pltpu.VMEM((6, 6, S, NZ), F32),
+            pltpu.VMEM(last.shape, BF),
             pltpu.VMEM((S, 8, FINE), BF),
-            dma((18,)),
+            dma((10,)),
             dma((7,)),
         ],
         compiler_params=pltpu.CompilerParams(vmem_limit_bytes=56 * 1024 * 1024),
         name="finish",
-    )(*between, *last, diffusion, box_pos, box_owner)
+    )(*between, last, diffusion)
     return jnp.transpose(coarse, (2, 0, 1, 3)), jnp.transpose(fine, (1, 0, 2))
 
 

time: 30.9 us -> 30.4 us (0.984)
  Pallas kernels: 30 us -> 29.5 us
    pallas_call x1, Pallas kernels: 3.23 us -> 2.72 us  [local(): pl.pallas_call(finish, out_shape=(jax.ShapeDtypeStruct((6, 6, S, NZ), F32...]
where the time goes in v3:
time: 30.4 us; the launch traced here: 30.2 us
  Pallas kernels  29.5 us (97%)
  between operations  0.64 us (2%)
    pallas_call x1, Pallas kernels, local(): pl.pallas_call(functools.partial(kernel, n_gx, n_yz), out_shape=tuple((ja...  26.8 us
    pallas_call x1, Pallas kernels, local(): pl.pallas_call(finish, out_shape=(jax.ShapeDtypeStruct((6, 6, S, NZ), F32...  2.72 us

profile of v3, /device:TPU:8, one launch (start us, length us, event | category | flops | bytes accessed | tf_op | source)
XLA Modules:
  0.0 30.2 jit_solution(2521096281928770664)
XLA Ops:
  0.6 26.8 %amr_step.1 = (f32[6,6,21,384]{3,2,1,0:T(8,128)}, f32[176,512]{1,0:T(8,128)}, bf16[8,16,128]{2,1,0:T(8,128)(2,1)}) custom-call(f32[6,6,21,384]{3,2,1,0:T(8,128)} %bitcast.4, bf16[21,8,512]{2,1,0:T(8,128)(2,1)} %bitcast.5, f32[21]{0:T(128)} %diffusion_in.3, f32[21,21]{1,0:T(8,128)} %rate_in.1, s32[1,1,4]{2,1,0:T(1,128)} %box_pos_in.1, ...), custom_call_target="tpu_custom_call" | custom-call | tf_op jit(solution)/shard_map/amr_step/pallas_call | solution.py:567
  27.5 2.7 %finish.1 = (f32[6,6,21,384]{3,2,1,0:T(8,128)}, bf16[21,8,512]{2,1,0:T(8,128)(2,1)}) custom-call(f32[6,6,21,384]{3,2,1,0:T(8,128)} %get-tuple-element.7.coarse_in, f32[176,512]{1,0:T(8,128)} %get-tuple-element.8.field_in, bf16[8,16,128]{2,1,0:T(8,128)(2,1)} %get-tuple-element.9.late_in, bf16[64,512]{1,0:T(8,128)(2,1)} %constant.29.clone.touch_in, f32[21]{0:T(128)} %diffusion_in.3), custom_call_target="tpu_custom_call" | custom-call | tf_op jit(solution)/shard_map/finish/pallas_call | solution.py:615

commit v4 on v3

--- a/solution.py
+++ b/solution.py
@@ -262,23 +262,19 @@
     to_down = remote(ysend.at[0], yrecv.at[1], halo_send, halo_recv, 2, (gx, down))
     to_up = remote(ysend.at[1], yrecv.at[0], halo_send, halo_recv, 3, (gx, up))
     slab(5)
-    pl.semaphore_wait(barrier, n_yz)
-    to_right.start()
-    pl.semaphore_signal(ready, inc=1, device_id=(right, me), device_id_type=mesh_id)
+
+    def enter():
+        pl.semaphore_wait(barrier, n_yz)
+        to_right.start()
+        pl.semaphore_signal(ready, inc=1, device_id=(right, me), device_id_type=mesh_id)
+
+    pl.when(gx == n_gx - 1)(enter)
     for x in range(5):
         slab(x)
     for pair in range(3):
         for side, part in ((0, slice(0, SP)), (1, slice(ROWS - SP, ROWS))):
             layers = [xf[2 * pair, part], xf[2 * pair + 1, part]]
             ysend[side, pair] = jnp.concatenate(layers, axis=0).astype(BF)
-    to_down.start()
-    to_up.start()
-
-    @pl.when(gx > 1)
-    def _():
-        pl.semaphore_wait(ready, 1)
-        to_left.start()
-
     for copy in small:
         copy.wait()
     rz[...] = jnp.zeros_like(rz)
@@ -373,7 +369,16 @@
     sent = sent + flag
     for owner in range(8):
         ghost_out[owner] = fold(for_owner(sent, owner), 64).astype(BF)
+    pl.when(gx != n_gx - 1)(enter)
     ghost_copies, own_ghost = exchange(ghost_out, ghost_in, ghost_send, ghost_recv, 0)
+    to_down.start()
+    to_up.start()
+
+    @pl.when(gx > 1)
+    def _():
+        pl.semaphore_wait(ready, 1)
+        to_left.start()
+
 
     for n in (0, 1, 2, 3):
         loads[n].wait()
@@ -444,11 +449,6 @@
         offset = zat - box_pos[0, 0, i] * 6
         inside = inside + jnp.where((offset >= 1) & (offset <= 4), 1, 0)
 
-    @pl.when(gx <= 1)
-    def _():
-        pl.semaphore_wait(ready, 1)
-        to_left.start()
-
     for n in (6, 7, 8, 9):
         loads[n].wait()
     delta = dot(patches, fixes[...])
@@ -467,6 +467,11 @@
         last = jnp.concatenate([part[16:24, :64], jnp.zeros((8, 64), F32)], axis=1)
         late_out[owner] = jnp.concatenate([first, last], axis=0).astype(BF)
     late_copies, own_late = exchange(late_out, late_got, late_send, late_recv, 2)
+
+    @pl.when(gx <= 1)
+    def _():
+        pl.semaphore_wait(ready, 1)
+        to_left.start()
 
     delta = d_box * (delta + d_box * dot(added.astype(BF), late[...]))
     for copy in back_copies:

time: 30.4 us -> 30.4 us (level)
  no operation moved by 1% of the time
where the time goes in v4:
time: 30.4 us; the launch traced here: 30.2 us
  Pallas kernels  29.5 us (97%)
  between operations  0.64 us (2%)
    pallas_call x1, Pallas kernels, local(): pl.pallas_call(functools.partial(kernel, n_gx, n_yz), out_shape=tuple((ja...  26.8 us
    pallas_call x1, Pallas kernels, local(): pl.pallas_call(finish, out_shape=(jax.ShapeDtypeStruct((6, 6, S, NZ), F32...  2.72 us

profile of v4, /device:TPU:8, one launch (start us, length us, event | category | flops | bytes accessed | tf_op | source)
XLA Modules:
  0.0 30.2 jit_solution(11410275440180817982)
XLA Ops:
  0.6 26.8 %amr_step.1 = (f32[6,6,21,384]{3,2,1,0:T(8,128)}, f32[176,512]{1,0:T(8,128)}, bf16[8,16,128]{2,1,0:T(8,128)(2,1)}) custom-call(f32[6,6,21,384]{3,2,1,0:T(8,128)} %bitcast.4, bf16[21,8,512]{2,1,0:T(8,128)(2,1)} %bitcast.5, f32[21]{0:T(128)} %diffusion_in.3, f32[21,21]{1,0:T(8,128)} %rate_in.1, s32[1,1,4]{2,1,0:T(1,128)} %box_pos_in.1, ...), custom_call_target="tpu_custom_call" | custom-call | tf_op jit(solution)/shard_map/amr_step/pallas_call | solution.py:572
  27.5 2.7 %finish.1 = (f32[6,6,21,384]{3,2,1,0:T(8,128)}, bf16[21,8,512]{2,1,0:T(8,128)(2,1)}) custom-call(f32[6,6,21,384]{3,2,1,0:T(8,128)} %get-tuple-element.7.coarse_in, f32[176,512]{1,0:T(8,128)} %get-tuple-element.8.field_in, bf16[8,16,128]{2,1,0:T(8,128)(2,1)} %get-tuple-element.9.late_in, bf16[64,512]{1,0:T(8,128)(2,1)} %constant.29.clone.touch_in, f32[21]{0:T(128)} %diffusion_in.3), custom_call_target="tpu_custom_call" | custom-call | tf_op jit(solution)/shard_map/finish/pallas_call | solution.py:620
